TPU v7x, 128 devices: a whole 4x4x4 slice. The times are simulated.
128 devices in a mesh: occ: 4 (over y_hi, core), aux: 32 (over x, z, y_lo).
Axes of the slice: x: 4, y: 4 (y_hi: 2, y_lo: 2; y = y_hi * 2 + y_lo), z: 4, core: 2. Of those that a mesh axis runs over, the one named last changes fastest.
Arguments:
- three_index: bfloat16 [12000, 6, 1920], P('aux'), may hold values from -0.47851562 to 0.47851562
- occ_energy: float32 [6], replicated, may hold values from -1.5 to -0.3
- vir_energy: float32 [1920], replicated, may hold values from 0.25 to 2.95
- batch_table: int32 [6], replicated, may hold values from 0 to 5, each once
- orbital_order: int32 [6], replicated, may hold values from 0 to 5, each once
- occ_pair_int: bfloat16 [2, 2, 12000], P(None, None, 'aux'), may hold values from -0.03881836 to 0.03881836
- half_ao: bfloat16 [2, 12000, 4000], P(None, 'aux'), may hold values from -9.536743e-06 to 9.536743e-06
- vir_coeff: bfloat16 [4000, 1920], P('aux', 'occ'), may hold values from -0.09375 to 0.09375
Outputs:
- gamma: bfloat16 [12000, 2, 1920], P('aux', None, 'occ')
- orbital_gradient: float32 [2, 1920], P(None, ('occ', 'aux'))
Inputs may be any that keep to these rules, and one draw needn't show every extreme that they name: `batch_table`: a permutation of 0 to 5; its first 4 entries are the partner orbitals of the window. `orbital_order`: a permutation of 0 to 5; its first 2 entries are the orbitals whose amplitudes are formed.
All inputs are finite; a program needn't handle non-finite values.
Results may differ from a plain program's by a relative error of at most 0.019.
Values may be sent and summed in bfloat16 or wider, within the bound.
No kernel may reach another device: no remote copies, remote signals or barrier semaphores. Data moves between devices by JAX's collectives and lax.ppermute only.
A program may use at most 128 MiB of HBM per device.

v0:
```python
import jax
import jax.numpy as jnp
from jax import lax
from jax.sharding import Mesh
from jax.sharding import PartitionSpec as P

NI = 2
KH = 2
ROWS = 30
PAD = 32
AUX = ("x", "z", "yl")
OCC_AUX = ("yh", "core", "x", "z", "yl")
F32 = jnp.float32
BF16 = jnp.bfloat16


def ring(n, d):
    return [(i, (i + d) % n) for i in range(n)]


def up(v, axis):
    return lax.ppermute(v, axis, ring(4, 1))


def down(v, axis):
    return lax.ppermute(v, axis, ring(4, -1))


def dot(a, b, dims):
    return lax.dot_general(a, b, (dims, ((), ())), preferred_element_type=F32)


def ring_sum(v, axis):
    lo2, hi2 = v[2]
    got_up = up(lo2.astype(BF16), axis)
    got_down = down(hi2.astype(BF16), axis)
    one = jnp.concatenate([v[1][0] + got_up.astype(F32), v[1][1]]).astype(BF16)
    three = jnp.concatenate([v[3][0], v[3][1] + got_down.astype(F32)]).astype(BF16)
    from_below = up(one, axis)
    from_above = down(three, axis)
    own = jnp.concatenate([v[0][0], v[0][1]])
    return own + from_below.astype(F32) + from_above.astype(F32)


def ring_gather(v, axis):
    below = up(v, axis)
    above = down(v, axis)
    half = v.shape[0] // 2
    lo = up(below[:half], axis)
    hi = down(above[half:], axis)
    return [v, above, jnp.concatenate([lo, hi]), below]


def local(
    three_index,
    occ_energy,
    vir_energy,
    batch_table,
    orbital_order,
    occ_pair_int,
    half_ao,
    vir_coeff,
):
    nq, _, nvirt = three_index.shape
    yh, core, x, z, yl = (lax.axis_index(a) for a in OCC_AUX)
    own_a = (yh * 2 + core) * (nvirt // 4)
    by_orbital = jnp.transpose(three_index, (1, 0, 2))

    def orbital(i):
        return lax.dynamic_index_in_dim(by_orbital, i, 0, keepdims=False)

    def partner_orbital(half, k):
        return lax.dynamic_index_in_dim(batch_table, half * KH + k, 0, keepdims=False)

    pairs = []
    for h in range(2):
        for c in range(2):
            for t in range(2):
                src = h * 4 + c * 2 + t
                dst = (h if c == 0 else 1 - h) * 4 + c * 2 + (1 - t)
                pairs.append((src, dst))
    swap = lambda v: lax.ppermute(v, ("yh", "core", "yl"), pairs)
    right_sent = orbital(partner_orbital(1 - yl, core))
    right_first = swap(right_sent)
    right_second = lax.ppermute(right_first, "core", [(0, 1), (1, 0)])
    place = lax.broadcasted_iota(jnp.int32, (16 * PAD, 1), 0)
    dx, dz, r = (place // (4 * PAD), place // PAD % 4, place % PAD)
    chunk = (x + dx) % 4 * 4 + (z + dz) % 4
    virt = jnp.where(r < ROWS, chunk * ROWS + r, -nvirt)

    def left_rows(first):
        hot = (lax.broadcasted_iota(jnp.int32, (1, nvirt), 1) == virt + first).astype(BF16)
        both = [
            dot(hot, orbital(orbital_order[s]), ((1,), (1,))).astype(BF16).reshape(16, 1, PAD, nq)
            for s in range(NI)
        ]
        return jnp.concatenate(both, axis=1).reshape(16 * NI * PAD, nq)

    target_yh = jnp.where(core == 0, yh, 1 - yh)
    left_own = left_rows(own_a)
    left_sent = left_rows((target_yh * 2 + core) * (nvirt // 4))
    left_other = swap(left_sent)
    right_own = [orbital(partner_orbital(yl, k)) for k in range(KH)]
    right_other = [
        jnp.where(core == 0, right_first, right_second),
        jnp.where(core == 0, right_second, right_first),
    ]
    pair_flat = occ_pair_int.reshape(NI * NI, nq)
    g = [dot(pair_flat, half_ao[t], ((1,), (0,))) for t in range(NI)]
    cell = lambda u, v, t: g[t][u * NI + v]
    fock_terms = []
    for s in range(NI):
        fock_terms.append(2.0 * cell(0, 0, s) - cell(s, 0, 0))
        fock_terms.append(2.0 * (cell(0, 1, s) + cell(1, 0, s)) - cell(s, 1, 0) - cell(s, 0, 1))
        fock_terms.append(2.0 * cell(1, 1, s) - cell(s, 1, 1))
    fock_terms = jnp.stack(fock_terms)
    n_aux = lax.axis_size(AUX)
    tile = half_ao.shape[2] // n_aux
    fock_tile = lax.psum_scatter(
        fock_terms.reshape(6, n_aux, tile).transpose(1, 0, 2), AUX, scatter_dimension=0, tiled=False
    )
    vir_part = jnp.dot(fock_tile, vir_coeff.astype(F32), precision=lax.Precision.HIGHEST)
    share = vir_part.shape[1] // n_aux
    vir_own = lax.psum_scatter(
        vir_part.reshape(6, n_aux, share).transpose(1, 0, 2), AUX, scatter_dimension=0, tiled=False
    )
    pair_other = lax.ppermute(pair_flat, "yl", [(0, 1), (1, 0)])
    z_part = jnp.stack(
        [
            dot(pair_flat, right_own[k], ((1,), (0,)))
            + dot(pair_other, right_other[k], ((1,), (0,)))
            for k in range(KH)
        ]
    )
    z_sum = lax.psum(z_part, ("x", "z"))

    def by_block(left, swapped):
        blocks = left.reshape(4, 4, NI * PAD, nq)
        blocks = blocks.transpose(1, 0, 2, 3) if swapped else blocks
        return blocks.reshape(4, 2, 2 * NI * PAD, nq)

    summed = []
    for k, (first, second) in enumerate((("x", "z"), ("z", "x"))):
        lo_, oo_ = (by_block(left_own, k == 1), by_block(left_other, k == 1))
        v = {}
        for d in (2, 1, 3, 0):
            v[d] = [
                dot(lo_[d, h], right_own[k], ((1,), (0,)))
                + dot(oo_[d, h], right_other[k], ((1,), (0,)))
                for h in range(2)
            ]
        u = ring_sum(v, first).reshape(4, 2, PAD, nvirt)
        w = ring_sum([[u[d, 0], u[d, 1]] for d in range(4)], second)
        summed.append(w.reshape(NI, PAD, nvirt))
    own_chunk = x * 4 + z
    padded = jnp.concatenate([vir_energy, vir_energy[:2]])
    row_energy = lax.dynamic_slice_in_dim(padded, own_a + own_chunk * ROWS, PAD)
    left_energy = jnp.stack([occ_energy[orbital_order[s]] for s in range(NI)])
    amps = []
    for k in range(KH):
        e_k = lax.dynamic_index_in_dim(occ_energy, partner_orbital(yl, k), 0, keepdims=False)
        denominator = (
            row_energy[None, :, None] + vir_energy[None, None, :] - left_energy[:, None, None] - e_k
        )
        amps.append((-summed[k] / denominator).astype(BF16))
    wide = [a.astype(F32) for a in amps]
    entries = [-sum((jnp.sum(w[s] * w[t]) for w in wide)) for s, t in ((0, 0), (0, 1), (1, 1))]
    density = lax.psum(jnp.stack(entries), OCC_AUX)
    occ_rows = []
    for s in range(NI):
        row = jnp.zeros((PAD,), F32)
        for k in range(KH):
            for u in range(NI):
                row = row - jnp.sum(wide[k][u] * z_sum[k, u * NI + s][None, :], axis=1)
        occ_rows.append(row)
    occ_rows = jnp.stack(occ_rows)
    mine = lax.dynamic_slice_in_dim(occ_rows, yl * share, share, axis=1)
    theirs = lax.dynamic_slice_in_dim(occ_rows, (1 - yl) * share, share, axis=1)
    occ_side = mine + lax.ppermute(theirs, "yl", [(0, 1), (1, 0)])
    gammas = []
    for k, (first, second) in enumerate((("z", "x"), ("x", "z"))):
        own = jnp.concatenate(ring_gather(amps[k].reshape(NI * PAD, nvirt), first))
        blocks = ring_gather(own, second)
        parts = [
            [dot(b, right[k], ((1,), (1,))) for b in blocks] for right in (right_other, right_own)
        ]
        both = [jnp.concatenate(p).reshape(4, 4, NI * PAD, nq) for p in parts]
        if k == 1:
            both = [b.transpose(1, 0, 2, 3) for b in both]
        gammas.append(both)
    gamma_sent = (gammas[0][0] + gammas[1][0]).astype(BF16)
    gamma_got = lax.ppermute(gamma_sent, "yl", [(0, 1), (1, 0)])
    gamma_rows = (gammas[0][1] + gammas[1][1] + gamma_got.astype(F32)).astype(BF16)
    gamma_rows = gamma_rows.reshape(16, NI, PAD, nq)
    target = lax.broadcasted_iota(jnp.int32, (nvirt // 4, 1), 0)
    back = (target == virt.reshape(1, 16 * PAD)).astype(BF16)
    gamma_out = jnp.stack(
        [
            dot(back, gamma_rows[:, s].reshape(16 * PAD, nq), ((1,), (0,))).astype(BF16)
            for s in range(NI)
        ]
    )
    gamma_out = jnp.transpose(gamma_out, (2, 0, 1))
    weights = vir_own.reshape(NI, 3, share)
    gradient = occ_side + jnp.sum(weights * density[None, :, None], axis=1)
    return (gamma_out, gradient)


def solution(mesh):
    torus = Mesh(mesh.devices.reshape(2, 2, 4, 4, 2), OCC_AUX)
    occ = ("yh", "core")
    return jax.shard_map(
        local,
        mesh=torus,
        in_specs=(
            P(AUX, None, None),
            P(),
            P(),
            P(),
            P(),
            P(None, None, AUX),
            P(None, AUX, None),
            P(AUX, occ),
        ),
        out_specs=(P(AUX, None, occ), P(None, OCC_AUX)),
        check_vma=False,
    )
```

profile of v0, /device:TPU:0, one launch (start us, length us, event | category | flops | bytes accessed | tf_op | source)
XLA Modules:
  0.0 838.8 jit_solution(4391718574668692102)
XLA Ops:
  10.5 2.6 dynamic-slice_bitcast_fusion
  18.5 2.5 fusion.101
  21.8 2.5 fusion.104
  26.4 1.9 collective-permute-start.36
  28.3 13.4 %fusion.165 = (bf16[1,375,4000]{2,0,1:T(2,128)(2,1)}, bf16[1,375,4000]{2,0,1:T(2,128)(2,1)}) fusion(bf16[2,375,4000]{2,0,1:T(2,128)(2,1)} %param.14), kind=kLoop, calls=%fused_computation.334 | loop fusion | bytes 12000000 | tf_op jit(solution)/shard_map/slice | solution.py:109
  41.7 13.8 %copy.135 = bf16[1,375,4000]{1,2,0:T(8,128)(2,1)S(1)} copy(bf16[1,375,4000]{2,0,1:T(2,128)(2,1)} %get-tuple-element.35) | data formatting | bytes 6000000
  56.4 13.9 %copy.134 = bf16[1,375,4000]{1,2,0:T(8,128)(2,1)S(1)} copy(bf16[1,375,4000]{2,0,1:T(2,128)(2,1)} %get-tuple-element.34) | data formatting | bytes 6000000
  74.2 2.5 fusion.95
  76.7 2.5 fusion.98
  80.5 2.8 fusion.79
  83.3 2.8 fusion.81
  86.0 2.7 fusion.77
  88.8 2.7 fusion.71
  91.5 2.7 fusion.73
  94.2 2.7 fusion.75
  97.0 2.8 fusion.83
  99.7 2.7 fusion.85
  104.5 2.7 fusion.53
  107.2 2.8 fusion.55
  111.6 2.8 fusion.51
  114.5 2.8 fusion.45
  117.3 2.7 fusion.47
  120.0 2.8 fusion.49
  122.8 2.8 fusion.59
  126.0 1.7 fusion.35
  128.4 2.8 fusion.57
  133.1 221.0 %all-reduce.4.cloned.1.call-done = f32[32,6,125]{2,1,0:T(8,128)} async-done(((f32[32,6,125]{2,1,0:T(8,128)}), f32[32,6,125]{2,1,0:T(8,128)}) %all-reduce.4.cloned.1.call-update) | async-done | bytes 96016
  354.1 1.8 convolution_bitcast_fusion
  356.1 154.6 %all-reduce.1 = f32[32,6,15]{2,1,0:T(8,128)S(1)} all-reduce(f32[32,6,15]{2,1,0:T(8,128)S(1)} %copy.133), channel_id=3, replica_groups=mesh['yh'=2,'core'=2,'x'=4,'z'=4,'yl'=2] {'x','z','yl'}, use_global_device_ids=true, to_apply=%region_10.11.clone | all-reduce | flops 2880 | bytes 23040
  513.6 2.3 broadcast_select_fusion
  519.9 3.2 collective-permute-start.5
  530.9 3.2 collective-permute-start.21
  537.5 70.3 %psum.14 = f32[2,4,1920]{2,1,0:T(4,128)S(1)} all-reduce(f32[2,4,1920]{2,1,0:T(4,128)S(1)} %pad_maximum_fusion.14), channel_id=1, replica_groups=mesh['yh'=2,'core'=2,'x'=4,'z'=4,'yl'=2] {'x','z'}, use_global_device_ids=true, to_apply=%region_0.1 | all-reduce | flops 15360 | bytes 122880 | tf_op jit(solution)/shard_map/psum | solution.py:135
  607.9 1.8 convolution_add_fusion.6
  614.1 2.3 collective-permute-start.6
  620.9 2.7 collective-permute-start.22
  623.5 3.2 collective-permute-done.4
  628.8 3.2 collective-permute-start.9
  632.1 1.8 collective-permute-done.20
  635.7 3.2 collective-permute-start.25
  639.1 3.8 collective-permute-start.10
  643.1 3.3 collective-permute-start.26
  646.9 3.5 collective-permute-done.24
  650.4 2.2 fusion.122
  654.3 3.3 collective-permute-start.27
  658.4 2.6 collective-permute-start.11
  668.1 65.9 %psum.15 = f32[3]{0:T(128)S(1)} all-reduce(f32[3]{0:T(128)S(1)} %pad_maximum_fusion.17), channel_id=1, replica_groups=mesh['yh'=2,'core'=2,'x'=4,'z'=4,'yl'=2] {'yh','core','x','z','yl'}, use_global_device_ids=true, to_apply=%region_17.18 | all-reduce | flops 3 | bytes 24 | tf_op jit(solution)/shard_map/psum | solution.py:168
  735.7 1.9 collective-permute-start.29
  740.9 1.9 collective-permute-start.13
  752.1 2.6 collective-permute-start.31
  758.3 2.7 collective-permute-start.15
  761.0 3.1 fusion.43
  764.1 2.9 fusion.69
  768.2 7.1 collective-permute-done.32
  775.6 3.3 collective-permute-start.34
  778.8 2.2 collective-permute-done.16
  782.7 3.2 collective-permute-start.18
  798.4 1.9 copy.122
  805.9 3.0 copy.121
  808.9 2.6 fusion.32
  813.0 2.0 fusion.39
  815.7 2.3 fusion.65
  819.5 1.9 copy.114
  821.3 6.9 collective-permute-done.35
  (282 shorter events, 98.1 us)
Async XLA Ops:
  7.2 7.6 copy-start.42
  7.2 347.0 %all-reduce.4.cloned.1.call-start = ((), (), s32[]{:S(2)}) async-start(), calls=%async_computation | async-start | bytes 262144
  13.1 112.5 %collective-permute-start.1 = (bf16[375,1920]{1,0:T(8,128)(2,1)}, bf16[375,1920]{1,0:T(8,128)(2,1)}, u32[]{:S(2)}, u32[]{:S(2)}) collective-permute-start(bf16[375,1920]{1,0:T(8,128)(2,1)} %dynamic-slice_bitcast_fusion), channel_id=1, source_target_pairs={{0,1},{1,0},{32,97},{33,96},{64,65},{65,64},{96,33},{97,32},{2,3},... | collective-permute-start | bytes 4320008 | tf_op jit(solution)/shard_map/ppermute | solution.py:82
  26.0 485.3 %collective-permute-start = (bf16[1024,375]{0,1:T(8,128)(2,1)}, bf16[1024,375]{0,1:T(8,128)(2,1)}, u32[]{:S(2)}, u32[]{:S(2)}) collective-permute-start(bf16[1024,375]{0,1:T(8,128)(2,1)} %copy.104), channel_id=1, source_target_pairs={{0,1},{1,0},{32,97},{33,96},{64,65},{65,64},{96,33},{97,32},{2,3},... | collective-permute-start | bytes 2304008 | tf_op jit(solution)/shard_map/ppermute | solution.py:82
  26.4 510.5 %collective-permute-start.36 = (bf16[4,375]{1,0:T(4,128)(2,1)S(1)}, bf16[4,375]{1,0:T(4,128)(2,1)S(1)}, u32[]{:S(2)}, u32[]{:S(2)}) collective-permute-start(bf16[4,375]{1,0:T(4,128)(2,1)S(1)} %reshape.436), channel_id=1, source_target_pairs={{0,1},{1,0},{2,3},{3,2},{4,5},{5,4},{6,7},{7,6},{8,9},{9,8},{10,11... | collective-permute-start | bytes 9008 | tf_op jit(solution)/shard_map/ppermute | solution.py:127
  122.8 3.0 copy-start.39
  122.8 3.1 slice-start.3
  122.8 4.9 copy-start.40
  125.6 388.0 %collective-permute-start.2 = (bf16[375,1920]{1,0:T(8,128)(2,1)}, bf16[375,1920]{1,0:T(8,128)(2,1)}, u32[]{:S(2)}, u32[]{:S(2)}) collective-permute-start(bf16[375,1920]{1,0:T(8,128)(2,1)} %collective-permute-done.1), channel_id=1, source_target_pairs={{0,32},{32,0},{1,33},{33,1},{2,34},{34,2},{3,35},{35,3},{4,36},{36... | collective-permute-start | bytes 4320008 | tf_op jit(solution)/shard_map/ppermute | solution.py:85
  127.7 4.8 copy-start.38
  127.7 4.9 copy-start.43
  513.6 21.9 %copy-start.25 = (bf16[4,4,64,375]{3,2,1,0:T(8,128)(2,1)}, bf16[4,4,64,375]{3,2,1,0:T(8,128)(2,1)S(1)}, u32[]{:S(2)}) copy-start(bf16[4,4,64,375]{3,2,1,0:T(8,128)(2,1)S(1)} %copy.118) | copy-start | bytes 2304004
  517.5 92.3 %collective-permute-start.3 = (bf16[128,1920]{1,0:T(8,128)(2,1)}, bf16[128,1920]{1,0:T(8,128)(2,1)}, u32[]{:S(2)}, u32[]{:S(2)}) collective-permute-start(bf16[128,1920]{1,0:T(8,128)(2,1)} %fusion.13), channel_id=1, source_target_pairs={{0,8},{8,16},{16,24},{24,0},{1,9},{9,17},{17,25},{25,1},{2,10},{10... | collective-permute-start | bytes 1474568 | tf_op jit(solution)/shard_map/ppermute | solution.py:22
  518.7 4.4 copy-start.13
  519.9 4.5 copy-start.12
  519.9 91.6 %collective-permute-start.5 = (bf16[128,1920]{1,0:T(8,128)(2,1)}, bf16[128,1920]{1,0:T(8,128)(2,1)}, u32[]{:S(2)}, u32[]{:S(2)}) collective-permute-start(bf16[128,1920]{1,0:T(8,128)(2,1)} %fusion.17), channel_id=1, source_target_pairs={{0,24},{8,0},{16,8},{24,16},{1,25},{9,1},{17,9},{25,17},{2,26},{10... | collective-permute-start | bytes 1474568 | tf_op jit(solution)/shard_map/ppermute | solution.py:26
  528.4 88.1 %collective-permute-start.19 = (bf16[128,1920]{1,0:T(8,128)(2,1)}, bf16[128,1920]{1,0:T(8,128)(2,1)}, u32[]{:S(2)}, u32[]{:S(2)}) collective-permute-start(bf16[128,1920]{1,0:T(8,128)(2,1)} %fusion.19), channel_id=1, source_target_pairs={{0,2},{2,4},{4,6},{6,0},{1,3},{3,5},{5,7},{7,1},{8,10},{10,12},{12... | collective-permute-start | bytes 1474568 | tf_op jit(solution)/shard_map/ppermute | solution.py:22
  529.7 4.5 copy-start.19
  530.9 4.7 copy-start.18
  530.9 87.7 %collective-permute-start.21 = (bf16[128,1920]{1,0:T(8,128)(2,1)}, bf16[128,1920]{1,0:T(8,128)(2,1)}, u32[]{:S(2)}, u32[]{:S(2)}) collective-permute-start(bf16[128,1920]{1,0:T(8,128)(2,1)} %fusion.23), channel_id=1, source_target_pairs={{0,6},{2,0},{4,2},{6,4},{1,7},{3,1},{5,3},{7,5},{8,14},{10,8},{12,... | collective-permute-start | bytes 1474568 | tf_op jit(solution)/shard_map/ppermute | solution.py:26
  611.4 15.4 %collective-permute-start.4 = (bf16[256,1920]{1,0:T(8,128)(2,1)S(1)}, bf16[256,1920]{1,0:T(8,128)(2,1)S(1)}, u32[]{:S(2)}, u32[]{:S(2)}) collective-permute-start(bf16[256,1920]{1,0:T(8,128)(2,1)S(1)} %pad_maximum_fusion.4), channel_id=1, source_target_pairs={{0,8},{8,16},{16,24},{24,0},{1,9},{9,17},{17,25},{25,1},{2,10},{10... | collective-permute-start | bytes 2949128 | tf_op jit(solution)/shard_map/ppermute | solution.py:22
  614.1 3.9 copy-start.27
  614.1 14.2 %collective-permute-start.6 = (bf16[256,1920]{1,0:T(8,128)(2,1)S(1)}, bf16[256,1920]{1,0:T(8,128)(2,1)S(1)}, u32[]{:S(2)}, u32[]{:S(2)}) collective-permute-start(bf16[256,1920]{1,0:T(8,128)(2,1)S(1)} %pad_maximum_fusion.5), channel_id=1, source_target_pairs={{0,24},{8,0},{16,8},{24,16},{1,25},{9,1},{17,9},{25,17},{2,26},{10... | collective-permute-start | bytes 2949128 | tf_op jit(solution)/shard_map/ppermute | solution.py:26
  618.1 2.7 copy-start.26
  618.1 15.8 %collective-permute-start.20 = (bf16[256,1920]{1,0:T(8,128)(2,1)S(1)}, bf16[256,1920]{1,0:T(8,128)(2,1)S(1)}, u32[]{:S(2)}, u32[]{:S(2)}) collective-permute-start(bf16[256,1920]{1,0:T(8,128)(2,1)S(1)} %pad_maximum_fusion.6), channel_id=1, source_target_pairs={{0,2},{2,4},{4,6},{6,0},{1,3},{3,5},{5,7},{7,1},{8,10},{10,12},{12... | collective-permute-start | bytes 2949128 | tf_op jit(solution)/shard_map/ppermute | solution.py:22
  620.8 7.6 copy-start.23
  620.8 7.5 copy-start.24
  620.9 14.3 %collective-permute-start.22 = (bf16[256,1920]{1,0:T(8,128)(2,1)S(1)}, bf16[256,1920]{1,0:T(8,128)(2,1)S(1)}, u32[]{:S(2)}, u32[]{:S(2)}) collective-permute-start(bf16[256,1920]{1,0:T(8,128)(2,1)S(1)} %pad_maximum_fusion.7), channel_id=1, source_target_pairs={{0,6},{2,0},{4,2},{6,4},{1,7},{3,1},{5,3},{7,5},{8,14},{10,8},{12,... | collective-permute-start | bytes 2949128 | tf_op jit(solution)/shard_map/ppermute | solution.py:26
  628.7 6.5 copy-start.20
  628.8 10.1 %collective-permute-start.7 = (bf16[32,1920]{1,0:T(8,128)(2,1)S(1)}, bf16[32,1920]{1,0:T(8,128)(2,1)S(1)}, u32[]{:S(2)}, u32[]{:S(2)}) collective-permute-start(bf16[32,1920]{1,0:T(8,128)(2,1)S(1)} %get-tuple-element.50), channel_id=1, source_target_pairs={{0,2},{2,4},{4,6},{6,0},{1,3},{3,5},{5,7},{7,1},{8,10},{10,12},{12... | collective-permute-start | bytes 368648 | tf_op jit(solution)/shard_map/ppermute | solution.py:22
  628.8 10.1 %collective-permute-start.9 = (bf16[32,1920]{1,0:T(8,128)(2,1)S(1)}, bf16[32,1920]{1,0:T(8,128)(2,1)S(1)}, u32[]{:S(2)}, u32[]{:S(2)}) collective-permute-start(bf16[32,1920]{1,0:T(8,128)(2,1)S(1)} %get-tuple-element.51), channel_id=1, source_target_pairs={{0,6},{2,0},{4,2},{6,4},{1,7},{3,1},{5,3},{7,5},{8,14},{10,8},{12,... | collective-permute-start | bytes 368648 | tf_op jit(solution)/shard_map/ppermute | solution.py:26
  635.6 7.3 collective-permute-start.23
  635.7 7.2 collective-permute-start.25
  639.0 7.9 collective-permute-start.8
  639.1 7.8 collective-permute-start.10
  643.0 7.5 collective-permute-start.24
  643.1 7.4 collective-permute-start.26
  654.3 83.3 %collective-permute-start.27 = (bf16[64,1920]{1,0:T(8,128)(2,1)}, bf16[64,1920]{1,0:T(8,128)(2,1)}, u32[]{:S(2)}, u32[]{:S(2)}) collective-permute-start(bf16[64,1920]{1,0:T(8,128)(2,1)} %get-tuple-element.30), channel_id=1, source_target_pairs={{0,24},{8,0},{16,8},{24,16},{1,25},{9,1},{17,9},{25,17},{2,26},{10... | collective-permute-start | bytes 737288 | tf_op jit(solution)/shard_map/ppermute | solution.py:26
  657.7 77.1 %collective-permute-start.28 = (bf16[64,1920]{1,0:T(8,128)(2,1)}, bf16[64,1920]{1,0:T(8,128)(2,1)}, u32[]{:S(2)}, u32[]{:S(2)}) collective-permute-start(bf16[64,1920]{1,0:T(8,128)(2,1)} %get-tuple-element.30), channel_id=1, source_target_pairs={{0,8},{8,16},{16,24},{24,0},{1,9},{9,17},{17,25},{25,1},{2,10},{10... | collective-permute-start | bytes 737288 | tf_op jit(solution)/shard_map/ppermute | solution.py:22
  658.4 84.4 %collective-permute-start.11 = (bf16[64,1920]{1,0:T(8,128)(2,1)S(1)}, bf16[64,1920]{1,0:T(8,128)(2,1)}, u32[]{:S(2)}, u32[]{:S(2)}) collective-permute-start(bf16[64,1920]{1,0:T(8,128)(2,1)S(1)} %get-tuple-element.58), channel_id=1, source_target_pairs={{0,6},{2,0},{4,2},{6,4},{1,7},{3,1},{5,3},{7,5},{8,14},{10,8},{12,... | collective-permute-start | bytes 737288 | tf_op jit(solution)/shard_map/ppermute | solution.py:26
  661.0 79.0 %collective-permute-start.12 = (bf16[64,1920]{1,0:T(8,128)(2,1)S(1)}, bf16[64,1920]{1,0:T(8,128)(2,1)}, u32[]{:S(2)}, u32[]{:S(2)}) collective-permute-start(bf16[64,1920]{1,0:T(8,128)(2,1)S(1)} %get-tuple-element.58), channel_id=1, source_target_pairs={{0,2},{2,4},{4,6},{6,0},{1,3},{3,5},{5,7},{7,1},{8,10},{10,12},{12... | collective-permute-start | bytes 737288 | tf_op jit(solution)/shard_map/ppermute | solution.py:22
  668.1 66.0 %collective-permute-start.37 = (f32[2,15]{1,0:T(2,128)S(1)}, f32[2,15]{1,0:T(2,128)S(1)}, u32[]{:S(2)}, u32[]{:S(2)}) collective-permute-start(f32[2,15]{1,0:T(2,128)S(1)} %constant_dynamic-slice_fusion), channel_id=1, source_target_pairs={{0,1},{1,0},{2,3},{3,2},{4,5},{5,4},{6,7},{7,6},{8,9},{9,8},{10,11... | collective-permute-start | bytes 368 | tf_op jit(solution)/shard_map/ppermute | solution.py:179
  735.7 12.8 %collective-permute-start.29 = (bf16[32,1920]{1,0:T(8,128)(2,1)S(1)}, bf16[32,1920]{1,0:T(8,128)(2,1)S(1)}, u32[]{:S(2)}, u32[]{:S(2)}) collective-permute-start(bf16[32,1920]{1,0:T(8,128)(2,1)S(1)} %slice.420), channel_id=1, source_target_pairs={{0,8},{8,16},{16,24},{24,0},{1,9},{9,17},{17,25},{25,1},{2,10},{10... | collective-permute-start | bytes 368648 | tf_op jit(solution)/shard_map/ppermute | solution.py:22
  738.5 10.6 %collective-permute-start.30 = (bf16[32,1920]{1,0:T(8,128)(2,1)S(1)}, bf16[32,1920]{1,0:T(8,128)(2,1)S(1)}, u32[]{:S(2)}, u32[]{:S(2)}) collective-permute-start(bf16[32,1920]{1,0:T(8,128)(2,1)S(1)} %slice.421), channel_id=1, source_target_pairs={{0,24},{8,0},{16,8},{24,16},{1,25},{9,1},{17,9},{25,17},{2,26},{10... | collective-permute-start | bytes 368648 | tf_op jit(solution)/shard_map/ppermute | solution.py:26
  740.9 13.8 %collective-permute-start.13 = (bf16[32,1920]{1,0:T(8,128)(2,1)S(1)}, bf16[32,1920]{1,0:T(8,128)(2,1)S(1)}, u32[]{:S(2)}, u32[]{:S(2)}) collective-permute-start(bf16[32,1920]{1,0:T(8,128)(2,1)S(1)} %slice.392), channel_id=1, source_target_pairs={{0,2},{2,4},{4,6},{6,0},{1,3},{3,5},{5,7},{7,1},{8,10},{10,12},{12... | collective-permute-start | bytes 368648 | tf_op jit(solution)/shard_map/ppermute | solution.py:22
  743.7 11.6 %collective-permute-start.14 = (bf16[32,1920]{1,0:T(8,128)(2,1)S(1)}, bf16[32,1920]{1,0:T(8,128)(2,1)S(1)}, u32[]{:S(2)}, u32[]{:S(2)}) collective-permute-start(bf16[32,1920]{1,0:T(8,128)(2,1)S(1)} %slice.393), channel_id=1, source_target_pairs={{0,6},{2,0},{4,2},{6,4},{1,7},{3,1},{5,3},{7,5},{8,14},{10,8},{12,... | collective-permute-start | bytes 368648 | tf_op jit(solution)/shard_map/ppermute | solution.py:26
  751.4 23.9 %collective-permute-start.32 = (bf16[256,1920]{1,0:T(8,128)(2,1)}, bf16[256,1920]{1,0:T(8,128)(2,1)S(1)}, u32[]{:S(2)}, u32[]{:S(2)}) collective-permute-start(bf16[256,1920]{1,0:T(8,128)(2,1)} %constant_dynamic-update-slice_fusion.7), channel_id=1, source_target_pairs={{0,2},{2,4},{4,6},{6,0},{1,3},{3,5},{5,7},{7,1},{8,10},{10,12},{12... | collective-permute-start | bytes 2949128 | tf_op jit(solution)/shard_map/ppermute | solution.py:22
  752.1 23.4 %collective-permute-start.31 = (bf16[256,1920]{1,0:T(8,128)(2,1)}, bf16[256,1920]{1,0:T(8,128)(2,1)S(1)}, u32[]{:S(2)}, u32[]{:S(2)}) collective-permute-start(bf16[256,1920]{1,0:T(8,128)(2,1)} %constant_dynamic-update-slice_fusion.7), channel_id=1, source_target_pairs={{0,6},{2,0},{4,2},{6,4},{1,7},{3,1},{5,3},{7,5},{8,14},{10,8},{12,... | collective-permute-start | bytes 2949128 | tf_op jit(solution)/shard_map/ppermute | solution.py:26
  757.6 6.5 copy-start.6
  757.6 23.4 %collective-permute-start.16 = (bf16[256,1920]{1,0:T(8,128)(2,1)}, bf16[256,1920]{1,0:T(8,128)(2,1)S(1)}, u32[]{:S(2)}, u32[]{:S(2)}) collective-permute-start(bf16[256,1920]{1,0:T(8,128)(2,1)} %constant_dynamic-update-slice_fusion), channel_id=1, source_target_pairs={{0,8},{8,16},{16,24},{24,0},{1,9},{9,17},{17,25},{25,1},{2,10},{10... | collective-permute-start | bytes 2949128 | tf_op jit(solution)/shard_map/ppermute | solution.py:22
  758.3 23.5 %collective-permute-start.15 = (bf16[256,1920]{1,0:T(8,128)(2,1)}, bf16[256,1920]{1,0:T(8,128)(2,1)S(1)}, u32[]{:S(2)}, u32[]{:S(2)}) collective-permute-start(bf16[256,1920]{1,0:T(8,128)(2,1)} %constant_dynamic-update-slice_fusion), channel_id=1, source_target_pairs={{0,24},{8,0},{16,8},{24,16},{1,25},{9,1},{17,9},{25,17},{2,26},{10... | collective-permute-start | bytes 2949128 | tf_op jit(solution)/shard_map/ppermute | solution.py:26
  761.0 6.0 copy-start.5
  764.1 25.7 %slice-start = ((s8[8663040]{0:T(1024)(128)(4,1)}), s8[4194304]{0:T(1024)(128)(4,1)S(1)}, s32[]{:S(2)}) async-start(s8[8663040]{0:T(1024)(128)(4,1)} %bitcast.415), calls=%async_computation.1 | async-start | bytes 8388608
  767.6 22.3 %slice-start.1 = ((s8[8663040]{0:T(1024)(128)(4,1)}), s8[4194304]{0:T(1024)(128)(4,1)S(1)}, s32[]{:S(2)}) async-start(s8[8663040]{0:T(1024)(128)(4,1)} %bitcast.415), calls=%async_computation.2 | async-start | bytes 8388608
  775.4 20.0 %collective-permute-start.33 = (bf16[128,1920]{1,0:T(8,128)(2,1)S(1)}, bf16[128,1920]{1,0:T(8,128)(2,1)S(1)}, u32[]{:S(2)}, u32[]{:S(2)}) collective-permute-start(bf16[128,1920]{1,0:T(8,128)(2,1)S(1)} %slice.422), channel_id=1, source_target_pairs={{0,2},{2,4},{4,6},{6,0},{1,3},{3,5},{5,7},{7,1},{8,10},{10,12},{12... | collective-permute-start | bytes 1474568 | tf_op jit(solution)/shard_map/ppermute | solution.py:22
  775.6 19.9 %collective-permute-start.34 = (bf16[128,1920]{1,0:T(8,128)(2,1)S(1)}, bf16[128,1920]{1,0:T(8,128)(2,1)S(1)}, u32[]{:S(2)}, u32[]{:S(2)}) collective-permute-start(bf16[128,1920]{1,0:T(8,128)(2,1)S(1)} %slice.423), channel_id=1, source_target_pairs={{0,6},{2,0},{4,2},{6,4},{1,7},{3,1},{5,3},{7,5},{8,14},{10,8},{12,... | collective-permute-start | bytes 1474568 | tf_op jit(solution)/shard_map/ppermute | solution.py:26
  781.8 18.4 %collective-permute-start.17 = (bf16[128,1920]{1,0:T(8,128)(2,1)}, bf16[128,1920]{1,0:T(8,128)(2,1)}, u32[]{:S(2)}, u32[]{:S(2)}) collective-permute-start(bf16[128,1920]{1,0:T(8,128)(2,1)} %slice.394), channel_id=1, source_target_pairs={{0,8},{8,16},{16,24},{24,0},{1,9},{9,17},{17,25},{25,1},{2,10},{10... | collective-permute-start | bytes 1474568 | tf_op jit(solution)/shard_map/ppermute | solution.py:22
  782.7 18.7 %collective-permute-start.18 = (bf16[128,1920]{1,0:T(8,128)(2,1)}, bf16[128,1920]{1,0:T(8,128)(2,1)}, u32[]{:S(2)}, u32[]{:S(2)}) collective-permute-start(bf16[128,1920]{1,0:T(8,128)(2,1)} %slice.395), channel_id=1, source_target_pairs={{0,24},{8,0},{16,8},{24,16},{1,25},{9,1},{17,9},{25,17},{2,26},{10... | collective-permute-start | bytes 1474568 | tf_op jit(solution)/shard_map/ppermute | solution.py:26
  786.5 3.4 slice-start.2
  808.9 4.1 copy-start.3
  811.5 3.5 copy-start.33
  811.5 3.5 copy-start.36
  811.5 3.5 copy-start.37
  811.5 16.8 %collective-permute-start.35 = (bf16[4,4,64,375]{3,2,1,0:T(8,128)(2,1)}, bf16[4,4,64,375]{3,2,1,0:T(8,128)(2,1)}, u32[]{:S(2)}, u32[]{:S(2)}) collective-permute-start(bf16[4,4,64,375]{3,2,1,0:T(8,128)(2,1)} %fusion.32), channel_id=1, source_target_pairs={{0,1},{1,0},{2,3},{3,2},{4,5},{5,4},{6,7},{7,6},{8,9},{9,8},{10,11... | collective-permute-start | bytes 2304008 | tf_op jit(solution)/shard_map/ppermute | solution.py:192
  (23 other events, 37.6 us)
Sparse Core Ops, SparseCore 0:
  73.1 280.9 all-reduce.3
where the time goes:
time: 845 us; the launch traced here: 839 us
  blocking collectives  291 us (34%)
  waiting for transfers between devices  249 us (29%)
  matrix products  107 us (13%)
  local copies, waits for them, and re-layouts  85.2 us (10%)
  starting transfers between devices  57.4 us (7%)
  between operations  28.5 us (3%)
  other arithmetic  21.1 us (2%)
    unnamed x2, waiting for transfers between devices  221 us
    unnamed x1, blocking collectives  155 us
    dot_general x60, matrix products, dot(): return lax.dot_general(a, b, (dims, ((), ())), preferred_element_type=F32)  105 us
    psum x1, blocking collectives, local(): z_sum = lax.psum(z_part, ('x', 'z'))  70.3 us
    psum x1, blocking collectives, local(): density = lax.psum(jnp.stack(entries), OCC_AUX)  65.9 us
    ppermute x16, starting transfers between devices, down(): return lax.ppermute(v, axis, ring(4, -1))  45.5 us
    unnamed x108, local copies, waits for them, and re-layouts  43.4 us
    ppermute x16, waiting for transfers between devices, up(): return lax.ppermute(v, axis, ring(4, 1))  18.4 us
  transfers between devices with their start and end apart: 39, of which 10 were waited for; matrix products, arithmetic and copies ran while one was open for 22% of the time, Pallas kernels for 0%

commit v1 on v0

--- a/solution.py
+++ b/solution.py
@@ -132,7 +132,7 @@
             for k in range(KH)
         ]
     )
-    z_sum = lax.psum(z_part, ("x", "z"))
+    z_sum = lax.psum(lax.psum(z_part, axis_name="z"), "x")
 
     def by_block(left, swapped):
         blocks = left.reshape(4, 4, NI * PAD, nq)

time: 845 us -> 811 us (0.960)
  blocking collectives: 291 us -> 256 us
    psum x1 -> x2, blocking collectives: 70.3 us -> 36 us  [local(): z_sum = lax.psum(lax.psum(z_part, axis_name='z'), 'x')]
  transfers between devices with their start and end apart: 39 -> 39, of which waited for: 10 -> 10; matrix products, arithmetic and copies ran while one was open for 22% -> 23% of each run, Pallas kernels for 0% -> 0%
where the time goes in v1:
time: 811 us; the launch traced here: 805 us
  blocking collectives  256 us (32%)
  waiting for transfers between devices  249 us (31%)
  matrix products  107 us (13%)
  local copies, waits for them, and re-layouts  84.8 us (10%)
  starting transfers between devices  58.1 us (7%)
  between operations  29 us (4%)
  other arithmetic  21.3 us (3%)
    unnamed x2, waiting for transfers between devices  221 us
    unnamed x1, blocking collectives  155 us
    dot_general x60, matrix products, dot(): return lax.dot_general(a, b, (dims, ((), ())), preferred_element_type=F32)  105 us
    psum x1, blocking collectives, local(): density = lax.psum(jnp.stack(entries), OCC_AUX)  65.8 us
    ppermute x16, starting transfers between devices, down(): return lax.ppermute(v, axis, ring(4, -1))  44.9 us
    unnamed x108, local copies, waits for them, and re-layouts  42.9 us
    psum x2, blocking collectives, local(): z_sum = lax.psum(lax.psum(z_part, axis_name='z'), 'x')  36 us
    ppermute x16, waiting for transfers between devices, up(): return lax.ppermute(v, axis, ring(4, 1))  18.6 us
  transfers between devices with their start and end apart: 39, of which 10 were waited for; matrix products, arithmetic and copies ran while one was open for 23% of the time, Pallas kernels for 0%

profile of v1, /device:TPU:0, one launch (start us, length us, event | category | flops | bytes accessed | tf_op | source)
XLA Modules:
  0.0 805.0 jit_solution(3090655464387811991)
XLA Ops:
  10.6 2.6 dynamic-slice_bitcast_fusion
  18.7 2.5 fusion.101
  22.1 2.5 fusion.104
  26.7 1.9 collective-permute-start.36
  28.6 13.4 %fusion.165 = (bf16[1,375,4000]{2,0,1:T(2,128)(2,1)}, bf16[1,375,4000]{2,0,1:T(2,128)(2,1)}) fusion(bf16[2,375,4000]{2,0,1:T(2,128)(2,1)} %param.14), kind=kLoop, calls=%fused_computation.334 | loop fusion | bytes 12000000 | tf_op jit(solution)/shard_map/slice | solution.py:109
  42.0 13.8 %copy.135 = bf16[1,375,4000]{1,2,0:T(8,128)(2,1)S(1)} copy(bf16[1,375,4000]{2,0,1:T(2,128)(2,1)} %get-tuple-element.35) | data formatting | bytes 6000000
  56.8 13.9 %copy.134 = bf16[1,375,4000]{1,2,0:T(8,128)(2,1)S(1)} copy(bf16[1,375,4000]{2,0,1:T(2,128)(2,1)} %get-tuple-element.34) | data formatting | bytes 6000000
  74.8 2.5 fusion.95
  77.3 2.5 fusion.98
  81.2 2.8 fusion.79
  84.0 2.7 fusion.81
  86.7 2.7 fusion.77
  89.5 2.7 fusion.71
  92.2 2.7 fusion.73
  94.9 2.7 fusion.75
  97.7 2.7 fusion.83
  100.4 2.7 fusion.85
  105.2 2.8 fusion.53
  107.9 2.8 fusion.55
  112.4 2.8 fusion.51
  115.2 2.8 fusion.45
  118.0 2.7 fusion.47
  120.7 2.8 fusion.49
  123.5 2.8 fusion.59
  129.1 2.7 fusion.57
  134.0 220.5 %all-reduce.4.cloned.1.call-done = f32[32,6,125]{2,1,0:T(8,128)} async-done(((f32[32,6,125]{2,1,0:T(8,128)}), f32[32,6,125]{2,1,0:T(8,128)}) %all-reduce.4.cloned.1.call-update) | async-done | bytes 96016
  354.5 1.9 convolution_bitcast_fusion
  356.5 154.6 %all-reduce.1 = f32[32,6,15]{2,1,0:T(8,128)S(1)} all-reduce(f32[32,6,15]{2,1,0:T(8,128)S(1)} %copy.133), channel_id=3, replica_groups=mesh['yh'=2,'core'=2,'x'=4,'z'=4,'yl'=2] {'x','z','yl'}, use_global_device_ids=true, to_apply=%region_11.12.clone | all-reduce | flops 2880 | bytes 23040
  514.1 2.3 broadcast_select_fusion
  520.4 3.2 collective-permute-start.5
  531.4 3.2 collective-permute-start.21
  537.9 21.0 %psum.21 = f32[2,4,1920]{2,1,0:T(4,128)S(1)} all-reduce(f32[2,4,1920]{2,1,0:T(4,128)S(1)} %pad_maximum_fusion.14), channel_id=1, replica_groups=mesh['yh'=2,'core'=2,'x'=4,'z'=4,'yl'=2] {'z'}, use_global_device_ids=true, to_apply=%region_0.1 | all-reduce | flops 15360 | bytes 122880 | tf_op jit(solution)/shard_map/psum | solution.py:135
  558.9 15.0 %psum.22 = f32[2,4,1920]{2,1,0:T(4,128)S(1)} all-reduce(f32[2,4,1920]{2,1,0:T(4,128)S(1)} %psum.21), channel_id=1, replica_groups=mesh['yh'=2,'core'=2,'x'=4,'z'=4,'yl'=2] {'x'}, use_global_device_ids=true, to_apply=%region_1.2 | all-reduce | flops 15360 | bytes 122880 | tf_op jit(solution)/shard_map/psum | solution.py:135
  574.1 1.8 convolution_add_fusion.6
  580.3 2.3 collective-permute-start.6
  587.0 2.7 collective-permute-start.22
  589.7 3.2 collective-permute-done.4
  595.0 3.2 collective-permute-start.9
  598.3 1.8 collective-permute-done.20
  601.8 3.2 collective-permute-start.25
  605.8 3.3 collective-permute-start.10
  609.2 3.3 collective-permute-start.26
  613.1 3.5 collective-permute-done.24
  616.6 2.3 fusion.122
  620.6 3.3 collective-permute-start.27
  624.6 2.6 collective-permute-start.11
  634.3 65.8 %psum.23 = f32[3]{0:T(128)S(1)} all-reduce(f32[3]{0:T(128)S(1)} %pad_maximum_fusion.17), channel_id=1, replica_groups=mesh['yh'=2,'core'=2,'x'=4,'z'=4,'yl'=2] {'yh','core','x','z','yl'}, use_global_device_ids=true, to_apply=%region_18.19 | all-reduce | flops 3 | bytes 24 | tf_op jit(solution)/shard_map/psum | solution.py:168
  701.8 1.9 collective-permute-start.29
  707.0 1.9 collective-permute-start.13
  718.2 2.6 collective-permute-start.31
  724.6 2.6 collective-permute-start.15
  727.2 3.1 fusion.43
  730.3 2.9 fusion.69
  734.4 7.1 collective-permute-done.32
  741.7 3.3 collective-permute-start.34
  745.0 2.4 collective-permute-done.16
  749.0 3.2 collective-permute-start.18
  764.7 1.9 copy.122
  772.2 3.0 copy.121
  775.2 2.6 fusion.32
  779.3 2.0 fusion.39
  782.0 2.3 fusion.65
  785.8 1.9 copy.114
  787.6 6.9 collective-permute-done.35
  (283 shorter events, 100.9 us)
Async XLA Ops:
  7.2 7.7 copy-start.42
  7.2 347.3 %all-reduce.4.cloned.1.call-start = ((), (), s32[]{:S(2)}) async-start(), calls=%async_computation | async-start | bytes 262144
  13.2 113.1 %collective-permute-start.1 = (bf16[375,1920]{1,0:T(8,128)(2,1)}, bf16[375,1920]{1,0:T(8,128)(2,1)}, u32[]{:S(2)}, u32[]{:S(2)}) collective-permute-start(bf16[375,1920]{1,0:T(8,128)(2,1)} %dynamic-slice_bitcast_fusion), channel_id=1, source_target_pairs={{0,1},{1,0},{32,97},{33,96},{64,65},{65,64},{96,33},{97,32},{2,3},... | collective-permute-start | bytes 4320008 | tf_op jit(solution)/shard_map/ppermute | solution.py:82
  26.3 485.4 %collective-permute-start = (bf16[1024,375]{0,1:T(8,128)(2,1)}, bf16[1024,375]{0,1:T(8,128)(2,1)}, u32[]{:S(2)}, u32[]{:S(2)}) collective-permute-start(bf16[1024,375]{0,1:T(8,128)(2,1)} %copy.104), channel_id=1, source_target_pairs={{0,1},{1,0},{32,97},{33,96},{64,65},{65,64},{96,33},{97,32},{2,3},... | collective-permute-start | bytes 2304008 | tf_op jit(solution)/shard_map/ppermute | solution.py:82
  26.7 510.6 %collective-permute-start.36 = (bf16[4,375]{1,0:T(4,128)(2,1)S(1)}, bf16[4,375]{1,0:T(4,128)(2,1)S(1)}, u32[]{:S(2)}, u32[]{:S(2)}) collective-permute-start(bf16[4,375]{1,0:T(4,128)(2,1)S(1)} %reshape.436), channel_id=1, source_target_pairs={{0,1},{1,0},{2,3},{3,2},{4,5},{5,4},{6,7},{7,6},{8,9},{9,8},{10,11... | collective-permute-start | bytes 9008 | tf_op jit(solution)/shard_map/ppermute | solution.py:127
  123.5 3.0 copy-start.39
  123.5 3.0 slice-start.3
  123.5 4.9 copy-start.40
  126.3 387.9 %collective-permute-start.2 = (bf16[375,1920]{1,0:T(8,128)(2,1)}, bf16[375,1920]{1,0:T(8,128)(2,1)}, u32[]{:S(2)}, u32[]{:S(2)}) collective-permute-start(bf16[375,1920]{1,0:T(8,128)(2,1)} %collective-permute-done.1), channel_id=1, source_target_pairs={{0,32},{32,0},{1,33},{33,1},{2,34},{34,2},{3,35},{35,3},{4,36},{36... | collective-permute-start | bytes 4320008 | tf_op jit(solution)/shard_map/ppermute | solution.py:85
  128.4 5.0 copy-start.38
  128.4 5.0 copy-start.43
  514.1 21.9 %copy-start.25 = (bf16[4,4,64,375]{3,2,1,0:T(8,128)(2,1)}, bf16[4,4,64,375]{3,2,1,0:T(8,128)(2,1)S(1)}, u32[]{:S(2)}) copy-start(bf16[4,4,64,375]{3,2,1,0:T(8,128)(2,1)S(1)} %copy.118) | copy-start | bytes 2304004
  518.0 57.9 %collective-permute-start.3 = (bf16[128,1920]{1,0:T(8,128)(2,1)}, bf16[128,1920]{1,0:T(8,128)(2,1)}, u32[]{:S(2)}, u32[]{:S(2)}) collective-permute-start(bf16[128,1920]{1,0:T(8,128)(2,1)} %fusion.13), channel_id=1, source_target_pairs={{0,8},{8,16},{16,24},{24,0},{1,9},{9,17},{17,25},{25,1},{2,10},{10... | collective-permute-start | bytes 1474568 | tf_op jit(solution)/shard_map/ppermute | solution.py:22
  519.2 4.5 copy-start.13
  520.4 4.5 copy-start.12
  520.4 57.9 %collective-permute-start.5 = (bf16[128,1920]{1,0:T(8,128)(2,1)}, bf16[128,1920]{1,0:T(8,128)(2,1)}, u32[]{:S(2)}, u32[]{:S(2)}) collective-permute-start(bf16[128,1920]{1,0:T(8,128)(2,1)} %fusion.17), channel_id=1, source_target_pairs={{0,24},{8,0},{16,8},{24,16},{1,25},{9,1},{17,9},{25,17},{2,26},{10... | collective-permute-start | bytes 1474568 | tf_op jit(solution)/shard_map/ppermute | solution.py:26
  528.9 53.7 %collective-permute-start.19 = (bf16[128,1920]{1,0:T(8,128)(2,1)}, bf16[128,1920]{1,0:T(8,128)(2,1)}, u32[]{:S(2)}, u32[]{:S(2)}) collective-permute-start(bf16[128,1920]{1,0:T(8,128)(2,1)} %fusion.19), channel_id=1, source_target_pairs={{0,2},{2,4},{4,6},{6,0},{1,3},{3,5},{5,7},{7,1},{8,10},{10,12},{12... | collective-permute-start | bytes 1474568 | tf_op jit(solution)/shard_map/ppermute | solution.py:22
  530.1 4.5 copy-start.20
  531.4 4.7 copy-start.18
  531.4 53.4 %collective-permute-start.21 = (bf16[128,1920]{1,0:T(8,128)(2,1)}, bf16[128,1920]{1,0:T(8,128)(2,1)}, u32[]{:S(2)}, u32[]{:S(2)}) collective-permute-start(bf16[128,1920]{1,0:T(8,128)(2,1)} %fusion.23), channel_id=1, source_target_pairs={{0,6},{2,0},{4,2},{6,4},{1,7},{3,1},{5,3},{7,5},{8,14},{10,8},{12,... | collective-permute-start | bytes 1474568 | tf_op jit(solution)/shard_map/ppermute | solution.py:26
  577.6 15.4 %collective-permute-start.4 = (bf16[256,1920]{1,0:T(8,128)(2,1)S(1)}, bf16[256,1920]{1,0:T(8,128)(2,1)S(1)}, u32[]{:S(2)}, u32[]{:S(2)}) collective-permute-start(bf16[256,1920]{1,0:T(8,128)(2,1)S(1)} %pad_maximum_fusion.4), channel_id=1, source_target_pairs={{0,8},{8,16},{16,24},{24,0},{1,9},{9,17},{17,25},{25,1},{2,10},{10... | collective-permute-start | bytes 2949128 | tf_op jit(solution)/shard_map/ppermute | solution.py:22
  580.3 3.8 copy-start.27
  580.3 14.2 %collective-permute-start.6 = (bf16[256,1920]{1,0:T(8,128)(2,1)S(1)}, bf16[256,1920]{1,0:T(8,128)(2,1)S(1)}, u32[]{:S(2)}, u32[]{:S(2)}) collective-permute-start(bf16[256,1920]{1,0:T(8,128)(2,1)S(1)} %pad_maximum_fusion.5), channel_id=1, source_target_pairs={{0,24},{8,0},{16,8},{24,16},{1,25},{9,1},{17,9},{25,17},{2,26},{10... | collective-permute-start | bytes 2949128 | tf_op jit(solution)/shard_map/ppermute | solution.py:26
  584.2 2.7 copy-start.26
  584.3 15.8 %collective-permute-start.20 = (bf16[256,1920]{1,0:T(8,128)(2,1)S(1)}, bf16[256,1920]{1,0:T(8,128)(2,1)S(1)}, u32[]{:S(2)}, u32[]{:S(2)}) collective-permute-start(bf16[256,1920]{1,0:T(8,128)(2,1)S(1)} %pad_maximum_fusion.6), channel_id=1, source_target_pairs={{0,2},{2,4},{4,6},{6,0},{1,3},{3,5},{5,7},{7,1},{8,10},{10,12},{12... | collective-permute-start | bytes 2949128 | tf_op jit(solution)/shard_map/ppermute | solution.py:22
  586.9 7.6 copy-start.23
  586.9 7.5 copy-start.24
  587.0 14.3 %collective-permute-start.22 = (bf16[256,1920]{1,0:T(8,128)(2,1)S(1)}, bf16[256,1920]{1,0:T(8,128)(2,1)S(1)}, u32[]{:S(2)}, u32[]{:S(2)}) collective-permute-start(bf16[256,1920]{1,0:T(8,128)(2,1)S(1)} %pad_maximum_fusion.7), channel_id=1, source_target_pairs={{0,6},{2,0},{4,2},{6,4},{1,7},{3,1},{5,3},{7,5},{8,14},{10,8},{12,... | collective-permute-start | bytes 2949128 | tf_op jit(solution)/shard_map/ppermute | solution.py:26
  594.9 6.5 copy-start.19
  594.9 10.1 %collective-permute-start.7 = (bf16[32,1920]{1,0:T(8,128)(2,1)S(1)}, bf16[32,1920]{1,0:T(8,128)(2,1)S(1)}, u32[]{:S(2)}, u32[]{:S(2)}) collective-permute-start(bf16[32,1920]{1,0:T(8,128)(2,1)S(1)} %get-tuple-element.50), channel_id=1, source_target_pairs={{0,2},{2,4},{4,6},{6,0},{1,3},{3,5},{5,7},{7,1},{8,10},{10,12},{12... | collective-permute-start | bytes 368648 | tf_op jit(solution)/shard_map/ppermute | solution.py:22
  595.0 10.1 %collective-permute-start.9 = (bf16[32,1920]{1,0:T(8,128)(2,1)S(1)}, bf16[32,1920]{1,0:T(8,128)(2,1)S(1)}, u32[]{:S(2)}, u32[]{:S(2)}) collective-permute-start(bf16[32,1920]{1,0:T(8,128)(2,1)S(1)} %get-tuple-element.51), channel_id=1, source_target_pairs={{0,6},{2,0},{4,2},{6,4},{1,7},{3,1},{5,3},{7,5},{8,14},{10,8},{12,... | collective-permute-start | bytes 368648 | tf_op jit(solution)/shard_map/ppermute | solution.py:26
  601.8 7.3 collective-permute-start.23
  601.8 7.2 collective-permute-start.25
  605.2 7.9 collective-permute-start.8
  605.8 7.3 collective-permute-start.10
  609.1 7.5 collective-permute-start.24
  609.2 7.4 collective-permute-start.26
  620.6 83.2 %collective-permute-start.27 = (bf16[64,1920]{1,0:T(8,128)(2,1)}, bf16[64,1920]{1,0:T(8,128)(2,1)}, u32[]{:S(2)}, u32[]{:S(2)}) collective-permute-start(bf16[64,1920]{1,0:T(8,128)(2,1)} %get-tuple-element.30), channel_id=1, source_target_pairs={{0,24},{8,0},{16,8},{24,16},{1,25},{9,1},{17,9},{25,17},{2,26},{10... | collective-permute-start | bytes 737288 | tf_op jit(solution)/shard_map/ppermute | solution.py:26
  623.9 77.0 %collective-permute-start.28 = (bf16[64,1920]{1,0:T(8,128)(2,1)}, bf16[64,1920]{1,0:T(8,128)(2,1)}, u32[]{:S(2)}, u32[]{:S(2)}) collective-permute-start(bf16[64,1920]{1,0:T(8,128)(2,1)} %get-tuple-element.30), channel_id=1, source_target_pairs={{0,8},{8,16},{16,24},{24,0},{1,9},{9,17},{17,25},{25,1},{2,10},{10... | collective-permute-start | bytes 737288 | tf_op jit(solution)/shard_map/ppermute | solution.py:22
  624.6 84.3 %collective-permute-start.11 = (bf16[64,1920]{1,0:T(8,128)(2,1)S(1)}, bf16[64,1920]{1,0:T(8,128)(2,1)}, u32[]{:S(2)}, u32[]{:S(2)}) collective-permute-start(bf16[64,1920]{1,0:T(8,128)(2,1)S(1)} %get-tuple-element.58), channel_id=1, source_target_pairs={{0,6},{2,0},{4,2},{6,4},{1,7},{3,1},{5,3},{7,5},{8,14},{10,8},{12,... | collective-permute-start | bytes 737288 | tf_op jit(solution)/shard_map/ppermute | solution.py:26
  627.2 78.9 %collective-permute-start.12 = (bf16[64,1920]{1,0:T(8,128)(2,1)S(1)}, bf16[64,1920]{1,0:T(8,128)(2,1)}, u32[]{:S(2)}, u32[]{:S(2)}) collective-permute-start(bf16[64,1920]{1,0:T(8,128)(2,1)S(1)} %get-tuple-element.58), channel_id=1, source_target_pairs={{0,2},{2,4},{4,6},{6,0},{1,3},{3,5},{5,7},{7,1},{8,10},{10,12},{12... | collective-permute-start | bytes 737288 | tf_op jit(solution)/shard_map/ppermute | solution.py:22
  634.3 66.0 %collective-permute-start.37 = (f32[2,15]{1,0:T(2,128)S(1)}, f32[2,15]{1,0:T(2,128)S(1)}, u32[]{:S(2)}, u32[]{:S(2)}) collective-permute-start(f32[2,15]{1,0:T(2,128)S(1)} %constant_dynamic-slice_fusion), channel_id=1, source_target_pairs={{0,1},{1,0},{2,3},{3,2},{4,5},{5,4},{6,7},{7,6},{8,9},{9,8},{10,11... | collective-permute-start | bytes 368 | tf_op jit(solution)/shard_map/ppermute | solution.py:179
  701.8 12.8 %collective-permute-start.29 = (bf16[32,1920]{1,0:T(8,128)(2,1)S(1)}, bf16[32,1920]{1,0:T(8,128)(2,1)S(1)}, u32[]{:S(2)}, u32[]{:S(2)}) collective-permute-start(bf16[32,1920]{1,0:T(8,128)(2,1)S(1)} %slice.420), channel_id=1, source_target_pairs={{0,8},{8,16},{16,24},{24,0},{1,9},{9,17},{17,25},{25,1},{2,10},{10... | collective-permute-start | bytes 368648 | tf_op jit(solution)/shard_map/ppermute | solution.py:22
  704.6 10.6 %collective-permute-start.30 = (bf16[32,1920]{1,0:T(8,128)(2,1)S(1)}, bf16[32,1920]{1,0:T(8,128)(2,1)S(1)}, u32[]{:S(2)}, u32[]{:S(2)}) collective-permute-start(bf16[32,1920]{1,0:T(8,128)(2,1)S(1)} %slice.421), channel_id=1, source_target_pairs={{0,24},{8,0},{16,8},{24,16},{1,25},{9,1},{17,9},{25,17},{2,26},{10... | collective-permute-start | bytes 368648 | tf_op jit(solution)/shard_map/ppermute | solution.py:26
  707.0 13.8 %collective-permute-start.13 = (bf16[32,1920]{1,0:T(8,128)(2,1)S(1)}, bf16[32,1920]{1,0:T(8,128)(2,1)S(1)}, u32[]{:S(2)}, u32[]{:S(2)}) collective-permute-start(bf16[32,1920]{1,0:T(8,128)(2,1)S(1)} %slice.392), channel_id=1, source_target_pairs={{0,2},{2,4},{4,6},{6,0},{1,3},{3,5},{5,7},{7,1},{8,10},{10,12},{12... | collective-permute-start | bytes 368648 | tf_op jit(solution)/shard_map/ppermute | solution.py:22
  709.8 11.7 %collective-permute-start.14 = (bf16[32,1920]{1,0:T(8,128)(2,1)S(1)}, bf16[32,1920]{1,0:T(8,128)(2,1)S(1)}, u32[]{:S(2)}, u32[]{:S(2)}) collective-permute-start(bf16[32,1920]{1,0:T(8,128)(2,1)S(1)} %slice.393), channel_id=1, source_target_pairs={{0,6},{2,0},{4,2},{6,4},{1,7},{3,1},{5,3},{7,5},{8,14},{10,8},{12,... | collective-permute-start | bytes 368648 | tf_op jit(solution)/shard_map/ppermute | solution.py:26
  717.6 23.9 %collective-permute-start.32 = (bf16[256,1920]{1,0:T(8,128)(2,1)}, bf16[256,1920]{1,0:T(8,128)(2,1)S(1)}, u32[]{:S(2)}, u32[]{:S(2)}) collective-permute-start(bf16[256,1920]{1,0:T(8,128)(2,1)} %constant_dynamic-update-slice_fusion.7), channel_id=1, source_target_pairs={{0,2},{2,4},{4,6},{6,0},{1,3},{3,5},{5,7},{7,1},{8,10},{10,12},{12... | collective-permute-start | bytes 2949128 | tf_op jit(solution)/shard_map/ppermute | solution.py:22
  718.2 23.4 %collective-permute-start.31 = (bf16[256,1920]{1,0:T(8,128)(2,1)}, bf16[256,1920]{1,0:T(8,128)(2,1)S(1)}, u32[]{:S(2)}, u32[]{:S(2)}) collective-permute-start(bf16[256,1920]{1,0:T(8,128)(2,1)} %constant_dynamic-update-slice_fusion.7), channel_id=1, source_target_pairs={{0,6},{2,0},{4,2},{6,4},{1,7},{3,1},{5,3},{7,5},{8,14},{10,8},{12,... | collective-permute-start | bytes 2949128 | tf_op jit(solution)/shard_map/ppermute | solution.py:26
  723.8 6.5 copy-start.6
  723.8 23.5 %collective-permute-start.16 = (bf16[256,1920]{1,0:T(8,128)(2,1)}, bf16[256,1920]{1,0:T(8,128)(2,1)S(1)}, u32[]{:S(2)}, u32[]{:S(2)}) collective-permute-start(bf16[256,1920]{1,0:T(8,128)(2,1)} %constant_dynamic-update-slice_fusion), channel_id=1, source_target_pairs={{0,8},{8,16},{16,24},{24,0},{1,9},{9,17},{17,25},{25,1},{2,10},{10... | collective-permute-start | bytes 2949128 | tf_op jit(solution)/shard_map/ppermute | solution.py:22
  724.6 23.5 %collective-permute-start.15 = (bf16[256,1920]{1,0:T(8,128)(2,1)}, bf16[256,1920]{1,0:T(8,128)(2,1)S(1)}, u32[]{:S(2)}, u32[]{:S(2)}) collective-permute-start(bf16[256,1920]{1,0:T(8,128)(2,1)} %constant_dynamic-update-slice_fusion), channel_id=1, source_target_pairs={{0,24},{8,0},{16,8},{24,16},{1,25},{9,1},{17,9},{25,17},{2,26},{10... | collective-permute-start | bytes 2949128 | tf_op jit(solution)/shard_map/ppermute | solution.py:26
  727.2 6.0 copy-start.5
  730.3 25.9 %slice-start = ((s8[8663040]{0:T(1024)(128)(4,1)}), s8[4194304]{0:T(1024)(128)(4,1)S(1)}, s32[]{:S(2)}) async-start(s8[8663040]{0:T(1024)(128)(4,1)} %bitcast.415), calls=%async_computation.1 | async-start | bytes 8388608
  733.8 22.4 %slice-start.1 = ((s8[8663040]{0:T(1024)(128)(4,1)}), s8[4194304]{0:T(1024)(128)(4,1)S(1)}, s32[]{:S(2)}) async-start(s8[8663040]{0:T(1024)(128)(4,1)} %bitcast.415), calls=%async_computation.2 | async-start | bytes 8388608
  741.6 20.1 %collective-permute-start.33 = (bf16[128,1920]{1,0:T(8,128)(2,1)S(1)}, bf16[128,1920]{1,0:T(8,128)(2,1)S(1)}, u32[]{:S(2)}, u32[]{:S(2)}) collective-permute-start(bf16[128,1920]{1,0:T(8,128)(2,1)S(1)} %slice.422), channel_id=1, source_target_pairs={{0,2},{2,4},{4,6},{6,0},{1,3},{3,5},{5,7},{7,1},{8,10},{10,12},{12... | collective-permute-start | bytes 1474568 | tf_op jit(solution)/shard_map/ppermute | solution.py:22
  741.7 20.0 %collective-permute-start.34 = (bf16[128,1920]{1,0:T(8,128)(2,1)S(1)}, bf16[128,1920]{1,0:T(8,128)(2,1)S(1)}, u32[]{:S(2)}, u32[]{:S(2)}) collective-permute-start(bf16[128,1920]{1,0:T(8,128)(2,1)S(1)} %slice.423), channel_id=1, source_target_pairs={{0,6},{2,0},{4,2},{6,4},{1,7},{3,1},{5,3},{7,5},{8,14},{10,8},{12,... | collective-permute-start | bytes 1474568 | tf_op jit(solution)/shard_map/ppermute | solution.py:26
  748.2 18.4 %collective-permute-start.17 = (bf16[128,1920]{1,0:T(8,128)(2,1)}, bf16[128,1920]{1,0:T(8,128)(2,1)}, u32[]{:S(2)}, u32[]{:S(2)}) collective-permute-start(bf16[128,1920]{1,0:T(8,128)(2,1)} %slice.394), channel_id=1, source_target_pairs={{0,8},{8,16},{16,24},{24,0},{1,9},{9,17},{17,25},{25,1},{2,10},{10... | collective-permute-start | bytes 1474568 | tf_op jit(solution)/shard_map/ppermute | solution.py:22
  749.0 18.7 %collective-permute-start.18 = (bf16[128,1920]{1,0:T(8,128)(2,1)}, bf16[128,1920]{1,0:T(8,128)(2,1)}, u32[]{:S(2)}, u32[]{:S(2)}) collective-permute-start(bf16[128,1920]{1,0:T(8,128)(2,1)} %slice.395), channel_id=1, source_target_pairs={{0,24},{8,0},{16,8},{24,16},{1,25},{9,1},{17,9},{25,17},{2,26},{10... | collective-permute-start | bytes 1474568 | tf_op jit(solution)/shard_map/ppermute | solution.py:26
  752.8 3.4 slice-start.2
  775.2 4.1 copy-start.3
  777.8 3.5 copy-start.33
  777.8 3.5 copy-start.36
  777.8 3.5 copy-start.37
  777.8 16.8 %collective-permute-start.35 = (bf16[4,4,64,375]{3,2,1,0:T(8,128)(2,1)}, bf16[4,4,64,375]{3,2,1,0:T(8,128)(2,1)}, u32[]{:S(2)}, u32[]{:S(2)}) collective-permute-start(bf16[4,4,64,375]{3,2,1,0:T(8,128)(2,1)} %fusion.32), channel_id=1, source_target_pairs={{0,1},{1,0},{2,3},{3,2},{4,5},{5,4},{6,7},{7,6},{8,9},{9,8},{10,11... | collective-permute-start | bytes 2304008 | tf_op jit(solution)/shard_map/ppermute | solution.py:192
  (23 other events, 37.6 us)
Sparse Core Ops, SparseCore 0:
  73.5 280.9 all-reduce.3
